TPU v7x, 32 devices: a whole 2x2x4 slice. The times are simulated.
32 devices in a mesh: row: 4 (over y, x), col: 8 (over z, core).
Axes of the slice: x: 2, y: 2, z: 4, core: 2. Of those that a mesh axis runs over, the one named last changes fastest.
Arguments:
- unfolding: float32 [1024, 4096], P('row', 'col'), may hold values from -40 to 40, as said below
- factor: float32 [1024, 64], replicated, may hold values from -6 to 6
Outputs:
- gram_lower: float32 [1024, 1024], P(('row', 'col'))
- new_factor: float32 [1024, 64], replicated
- core: float32 [64, 4096], P('row', 'col')
Inputs may be any that keep to these rules, and one draw needn't show every extreme that they name: Entries of the unfolding are real values.
All inputs are finite; a program needn't handle non-finite values.
Results may differ from a plain program's by a relative error of at most 0.0003.
Values sent between devices are 32-bit elements; how exact they have to be, the bound alone decides.
No kernel may reach another device: no remote copies, remote signals or barrier semaphores. Data moves between devices by JAX's collectives and lax.ppermute only.
A program may use at most 64 MiB of HBM per device.

v0:
```python
import math

import jax
import jax.numpy as jnp
from jax import lax
from jax.sharding import PartitionSpec as P


def orthonormal(image, mode):
    highest = lax.Precision.HIGHEST
    inner = jnp.dot(image.T, image, precision=highest, preferred_element_type=jnp.float32) / mode
    chol = jnp.linalg.cholesky(inner)
    return jax.scipy.linalg.solve_triangular(chol, image.T, lower=True).T


def body(unfolding, factor):
    highest = lax.Precision.HIGHEST
    n_row = lax.axis_size("row")
    n_col = lax.axis_size("col")
    devices = n_row * n_col
    regrouped = lax.all_to_all(unfolding, "row", split_axis=1, concat_axis=0, tiled=True)
    mode = regrouped.shape[0]
    total_cols = regrouped.shape[1] * devices
    half = mode // (2 * devices)
    partial_value = (
        lax.dot_general(
            regrouped,
            regrouped,
            (((1,), (1,)), ((), ())),
            precision=highest,
            preferred_element_type=jnp.float32,
        )
        / total_cols
    )
    blocks = partial_value.reshape(2 * devices, half, mode)
    first_half = blocks[:devices]
    second_half = blocks[devices:][::-1]
    owner = lax.axis_index(("row", "col"))
    local_rows = lax.broadcasted_iota(jnp.int32, (2 * half, mode), 0)
    local_cols = lax.broadcasted_iota(jnp.int32, (2 * half, mode), 1)
    source = jnp.where(
        local_rows < half,
        owner * half + local_rows,
        (2 * devices - 1 - owner) * half + local_rows - half,
    )
    width = (2 * devices + 1) * half
    first_ext = jnp.pad(first_half, ((0, 0), (0, 0), (0, half)))
    flipped = jnp.pad(second_half, ((0, 0), (0, 0), (0, half)))[:, :, ::-1]
    target = lax.broadcasted_iota(jnp.int32, (devices, half, width), 0)
    column = lax.broadcasted_iota(jnp.int32, (devices, half, width), 2)
    packed = jnp.where(column < (target + 1) * half, first_ext, flipped).reshape(
        devices * half, width
    )
    received = lax.psum_scatter(packed, ("row", "col"), scatter_dimension=0, tiled=True)
    mine = jnp.concatenate([received[:, :mode], received[:, ::-1][:, :mode]], axis=0)
    gram_lower = jnp.where(local_cols <= source, mine, jnp.float32(0.0))
    projected = lax.dot_general(
        regrouped,
        factor,
        (((0,), (0,)), ((), ())),
        precision=highest,
        preferred_element_type=jnp.float32,
    )
    term = (
        jnp.dot(regrouped, projected, precision=highest, preferred_element_type=jnp.float32)
        / total_cols
    )
    image = lax.psum(term, ("row", "col"))
    new_factor = orthonormal(image, mode)
    scale = 1.0 / math.sqrt(mode)
    rows_here = unfolding.shape[0]
    factor_here = lax.dynamic_slice_in_dim(
        new_factor, lax.axis_index("row") * rows_here, rows_here, 0
    )
    core = lax.psum_scatter(
        lax.dot_general(
            factor_here,
            unfolding,
            (((0,), (0,)), ((), ())),
            precision=highest,
            preferred_element_type=jnp.float32,
        )
        * scale,
        "row",
        scatter_dimension=0,
        tiled=True,
    )
    return (gram_lower, new_factor, core)


def solution(mesh):
    in_specs = (P("row", "col"), P())
    out_specs = (P(("row", "col"), None), P(), P("row", "col"))
    return jax.shard_map(body, mesh=mesh, in_specs=in_specs, out_specs=out_specs, check_vma=False)
```

profile of v0, /device:TPU:0, one launch (start us, length us, event | category | flops | bytes accessed | tf_op | source)
XLA Modules:
  0.0 291.3 jit_solution(963261788813044592)
XLA Ops:
  7.2 0.0 copy-start
  7.2 2.1 copy.7
  9.3 5.2 %all-to-all-start = ((f32[256,4,128]{0,2,1:T(8,128)}), f32[256,4,128]{0,2,1:T(8,128)S(1)}, u32[]{:S(2)}, u32[]{:S(2)}) async-start(f32[256,4,128]{0,2,1:T(8,128)} %bitcast), calls=%async_computation | async-start | bytes 1048576 | tf_op jit(solution)/shard_map/all_to_all | solution.py:21
  14.4 8.0 %all-to-all-done = f32[256,4,128]{0,2,1:T(8,128)S(1)} async-done(((f32[256,4,128]{0,2,1:T(8,128)}), f32[256,4,128]{0,2,1:T(8,128)S(1)}, u32[]{:S(2)}, u32[]{:S(2)}) %all-to-all-start) | async-done | bytes 524320 | tf_op jit(solution)/shard_map/all_to_all | solution.py:21
  22.4 0.2 copy.8
  22.6 5.0 %convolution_multiply_fusion = f32[1024,1024]{1,0:T(8,128)} fusion(f32[1024,128]{1,0:T(8,128)S(1)} %bitcast.28), kind=kOutput, calls=%fused_computation.2 | convolution fusion | flops 1611661312 | bytes 4718592 | tf_op jit(solution)/shard_map/dot_general | solution.py:26
  27.6 0.4 fusion.9
  28.0 1.4 fusion
  29.4 0.0 all-reduce.4.cloned.1.call-update
  29.5 0.0 reduce-scatter.3.cloned.1.call-start
  29.5 4.8 %fusion.7 = (f32[512,1024]{1,0:T(8,128)}, f32[512,1024]{1,0:T(8,128)}) fusion(f32[1024,1024]{1,0:T(8,128)} %convolution_multiply_fusion), kind=kLoop, calls=%fused_computation.24 | loop fusion | bytes 8388608 | tf_op jit(solution)/shard_map/slice | solution.py:36
  34.3 1.8 rev.7
  36.1 1.6 pad.8
  37.7 5.5 %reverse.1 = f32[32,16,1152]{2,1,0:T(8,128)S(1)} reverse(f32[32,16,1152]{2,1,0:T(8,128)} %bitcast.32), dimensions={2} | reverse | bytes 4718592
  43.1 3.8 %pad_select_fusion = f32[32,16,1040]{2,1,0:T(8,128)} fusion(f32[32,16,1024]{2,1,0:T(8,128)} %bitcast.33, s32[32]{0:T(128)S(1)} %add_multiply_fusion, f32[32,16,1152]{2,1,0:T(8,128)S(1)} %reverse.1), kind=kLoop, calls=%fused_computation | loop fusion | flops 1064960 | bytes 6357120 | tf_op jit(solution)/shard_map/jit(_where)/select_n | solution.py:51
  46.9 0.0 reduce-scatter.3.cloned.1.call-update
  46.9 0.0 reduce-scatter.5.cloned.1.call-start
  47.0 107.8 %all-reduce.4.cloned.1.call-done = f32[1024,64]{0,1:T(8,128)} async-done(((f32[1024,64]{0,1:T(8,128)}), f32[1024,64]{0,1:T(8,128)}) %all-reduce.4.cloned.1.call-update) | async-done | bytes 262160 | tf_op jit(solution)/shard_map/psum | solution.py:68
  154.9 1.4 fusion.10
  156.2 0.1 copy.9
  156.3 5.8 %cholesky.16 = f32[64,64]{1,0:T(8,128)S(1)} custom-call(f32[64,64]{1,0:T(8,128)S(1)} %fusion.5), custom_call_target="Cholesky" | custom-call | tf_op jit(solution)/shard_map/jit(cholesky)/cholesky | solution.py:12
  162.2 0.6 compare_reduce_fusion
  162.9 0.7 fusion.2
  163.5 4.9 %custom-call.7 = f32[1,64,64]{1,2,0:T(8,128)S(1)} custom-call(f32[1,64,64]{2,1,0:T(8,128)S(1)} %fusion.2), custom_call_target="InvertDiagBlocksLowerTriangular" | custom-call | tf_op jit(solution)/shard_map/jit(_solve_triangular)/triangular_solve | solution.py:13
  168.4 1.4 fusion.3
  169.8 1.1 convolution_multiply_fusion.2
  170.9 0.0 reduce-scatter.5.cloned.1.call-update
  171.0 87.4 %reduce-scatter.3.cloned.1.call-done = f32[16,1040]{1,0:T(8,128)} async-done(((f32[512,1040]{1,0:T(8,128)}), f32[16,1040]{1,0:T(8,128)}) %reduce-scatter.3.cloned.1.call-update) | async-done | bytes 66576 | tf_op jit(solution)/shard_map/reduce_scatter | solution.py:54
  258.3 1.0 fusion.8
  259.4 0.6 slice.39
  260.0 0.8 maximum_select_fusion
  260.7 24.0 %reduce-scatter.5.cloned.1.call-done = f32[16,512]{1,0:T(8,128)} async-done(((f32[64,512]{1,0:T(8,128)}), f32[16,512]{1,0:T(8,128)}) %reduce-scatter.5.cloned.1.call-update) | async-done | bytes 32784 | tf_op jit(solution)/shard_map/reduce_scatter | solution.py:75
  (11 shorter events, 0.1 us)
Async XLA Ops:
  7.2 20.4 %copy-start = (f32[1024,64]{0,1:T(8,128)S(1)}, f32[1024,64]{0,1:T(8,128)}, u32[]{:S(2)}) copy-start(f32[1024,64]{0,1:T(8,128)} %param.3) | copy-start | bytes 786436
  9.3 13.2 %all-to-all-start = ((f32[256,4,128]{0,2,1:T(8,128)}), f32[256,4,128]{0,2,1:T(8,128)S(1)}, u32[]{:S(2)}, u32[]{:S(2)}) async-start(f32[256,4,128]{0,2,1:T(8,128)} %bitcast), calls=%async_computation | async-start | bytes 1048576 | tf_op jit(solution)/shard_map/all_to_all | solution.py:21
  14.4 140.4 %all-reduce.4.cloned.1.call-start = ((), (), s32[]{:S(2)}) async-start(), calls=%async_computation.4 | async-start | bytes 524288 | tf_op jit(solution)/shard_map/psum | solution.py:68
  29.5 228.9 %reduce-scatter.3.cloned.1.call-start = ((), (), s32[]{:S(2)}) async-start(), calls=%async_computation.3 | async-start | bytes 2433024 | tf_op jit(solution)/shard_map/reduce_scatter | solution.py:54
  46.9 122.9 %copy-start.1 = (f32[256,512]{1,0:T(8,128)S(1)}, f32[256,512]{1,0:T(8,128)}, u32[]{:S(2)}) copy-start(f32[256,512]{1,0:T(8,128)} %param.2) | copy-start | bytes 1572868
  46.9 237.8 %reduce-scatter.5.cloned.1.call-start = ((), (), s32[]{:S(2)}) async-start(), calls=%async_computation.5 | async-start | bytes 163840 | tf_op jit(solution)/shard_map/reduce_scatter | solution.py:75
  169.8 114.9 %copy-start.2 = (f32[1024,64]{0,1:T(8,128)}, f32[1024,64]{0,1:T(8,128)S(1)}, u32[]{:S(2)}) copy-start(f32[1024,64]{0,1:T(8,128)S(1)} %fusion.3) | copy-start | bytes 786436
Sparse Core Ops, SparseCore 0:
  29.6 125.2 all-reduce.3
  160.1 98.1 reduce-scatter.2
  261.9 22.7 reduce-scatter.4
where the time goes:
time: 292 us; the launch traced here: 291 us
  waiting for transfers between devices  227 us (78%)
  local copies, waits for them, and re-layouts  17.6 us (6%)
  other arithmetic  16.6 us (6%)
  between operations  13.8 us (5%)
  matrix products  10.7 us (4%)
  starting transfers between devices  5.25 us (2%)
    psum x1, waiting for transfers between devices, body(): image = lax.psum(term, ('row', 'col'))  108 us
    reduce_scatter x1, waiting for transfers between devices, body(): lax.psum_scatter(packed, ('row', 'col'), scatter_dimension=0, tiled=True)  87.4 us
    reduce_scatter x1, waiting for transfers between devices, body(): lax.psum_scatter(lax.dot_general(factor_here, unfolding, (((0,), (0,)), (...  24 us
    all_to_all x1, waiting for transfers between devices, body(): lax.all_to_all(unfolding, 'row', split_axis=1, concat_axis=0, tiled=True)  8.01 us
    unnamed x8, local copies, waits for them, and re-layouts  7.55 us
    another operation x3, other arithmetic, orthonormal(): chol = jnp.linalg.cholesky(inner)  6.52 us
  transfers between devices with their start and end apart: 4, of which 4 were waited for; matrix products, arithmetic and copies ran while one was open for 12% of the time, Pallas kernels for 0%

commit v1 on v0

v1 whole, which is shorter than its diff:
```python
import math

import jax
import jax.numpy as jnp
from jax import lax
from jax.sharding import PartitionSpec as P

HIGH = lax.Precision.HIGH
HIGHEST = lax.Precision.HIGHEST


def partner_pairs(n, s):
    if n & (n - 1) == 0:
        return [(i, i ^ s) for i in range(n)]
    return [(i, (i + s) % n) for i in range(n)]


def partner_source(me, n, s):
    if n & (n - 1) == 0:
        return me ^ s
    return (me + n - s) % n


def gather_blocks(x, axis):
    n = lax.axis_size(axis)
    return [x] + [lax.ppermute(x, axis, partner_pairs(n, s)) for s in range(1, n)]


def dot(a, b, dims, precision=HIGH):
    return lax.dot_general(a, b, (dims, ((), ())), precision=precision, preferred_element_type=jnp.float32)


def body(unfolding, factor):
    n_row = lax.axis_size("row")
    n_col = lax.axis_size("col")
    row = lax.axis_index("row")
    col = lax.axis_index("col")
    rows_here, cols_here = unfolding.shape
    mode = rows_here * n_row
    rank = factor.shape[1]
    total_cols = cols_here * n_col
    group = mode // (2 * n_row)
    half = group // n_col

    blocks = gather_blocks(unfolding, "row")
    x = jnp.zeros((mode, cols_here), jnp.float32)
    for s, block in enumerate(blocks):
        x = lax.dynamic_update_slice(x, block, (partner_source(row, n_row, s) * rows_here, 0))

    y = dot(factor, x, ((0,), (0,)))
    term = dot(y, x, ((1,), (1,))) * (1.0 / total_cols)
    pieces = term.reshape(rank, n_col, mode // n_col).transpose(1, 0, 2)
    swapped = lax.all_to_all(pieces, "col", split_axis=0, concat_axis=0, tiled=True)
    part = jnp.sum(swapped, axis=0)
    image_t = jnp.zeros((rank, mode), jnp.float32)
    for s, block in enumerate(gather_blocks(part, "col")):
        image_t = lax.dynamic_update_slice(image_t, block, (0, partner_source(col, n_col, s) * (mode // n_col)))

    inner = dot(image_t, image_t, ((1,), (1,)), HIGHEST) / mode
    chol = jnp.linalg.cholesky(inner)
    factor_t = jax.scipy.linalg.solve_triangular(chol, image_t, lower=True)
    new_factor = factor_t.T
    rank_here = rank // n_row
    mine = lax.dynamic_slice_in_dim(factor_t, row * rank_here, rank_here, 0)
    core = dot(mine, x, ((1,), (0,))) * (1.0 / math.sqrt(mode))

    low = lax.dynamic_slice_in_dim(x, row * group, group, 0)
    high_start = mode - (row + 1) * group
    high = lax.dynamic_slice_in_dim(x, high_start, group, 0)
    high = high.reshape(n_col, half, cols_here)[::-1].reshape(group, cols_here)
    both = dot(jnp.concatenate([high, low], 0), x, ((1,), (1,))) * (1.0 / total_cols)
    width = mode + group
    split = mode - row * group
    column = lax.broadcasted_iota(jnp.int32, (group, width), 1)
    wide_high = jnp.pad(both[:group], ((0, 0), (0, group)))
    doubled = jnp.concatenate([both[group:], both[group:], both[group:, :group]], 1)
    rolled = lax.dynamic_slice_in_dim(doubled, row * group, width, 1)
    packed = jnp.where(column < split, wide_high, rolled)
    received = lax.all_to_all(packed.reshape(n_col, half, width), "col", split_axis=0, concat_axis=0, tiled=True)
    return finish(received, x, new_factor, core, split, half, group, mode, n_col, col, row)


def finish(received, x, new_factor, core, split, half, group, mode, n_col, col, row):
    total = jnp.sum(received, axis=0)
    low_cols = lax.dynamic_slice_in_dim(jnp.pad(total, ((0, 0), (0, mode))), split, mode, 1)
    owner = row * n_col + col
    r = lax.broadcasted_iota(jnp.int32, (half, mode), 0)
    c = lax.broadcasted_iota(jnp.int32, (half, mode), 1)
    low_row = owner * half + r
    high_row = mode - (owner + 1) * half + r
    gram_lower = jnp.concatenate(
        [
            jnp.where(c <= low_row, low_cols, 0.0),
            jnp.where(c <= high_row, total[:, :mode], 0.0),
        ],
        0,
    )
    return gram_lower, new_factor, core


def solution(mesh):
    in_specs = (P("row", "col"), P())
    out_specs = (P(("row", "col"), None), P(), P("row", "col"))
    return jax.shard_map(body, mesh=mesh, in_specs=in_specs, out_specs=out_specs, check_vma=False)
```

time: 292 us -> 89.2 us (0.31)
  waiting for transfers between devices: 227 us -> 39.5 us
  starting transfers between devices: 5.25 us -> 23.9 us
  local copies, waits for them, and re-layouts: 17.6 us -> 3.53 us
  between operations: 13.8 us -> 0.89 us
  matrix products: 10.7 us -> 6.04 us
    reduce_scatter x2 -> x0, waiting for transfers between devices: 111 us -> none  [the longest x1 87.4 us: body(): lax.psum_scatter(packed, ('row', 'col'), scatter_dimension=0, tiled=True)]
    psum x1 -> x0, waiting for transfers between devices: 108 us -> none  [body(): image = lax.psum(term, ('row', 'col'))]
    ppermute x0 -> x10, waiting for transfers between devices: none -> 30.6 us  [gather_blocks(): lax.ppermute(x, axis, partner_pairs(n, s))]
    ppermute x0 -> x10, starting transfers between devices: none -> 15.5 us  [gather_blocks(): lax.ppermute(x, axis, partner_pairs(n, s))]
    unnamed x8 -> x6, local copies, waits for them, and re-layouts: 7.55 us -> 0.02 us
    slice x3 -> x2, local copies, waits for them, and re-layouts: 6.42 us -> 0.08 us  [the longest x1 0.07 us: body(): wide_high = jnp.pad(both[:group], ((0, 0), (0, group)))]
    dot_general x5, matrix products: 9.27 us -> 5.61 us  [dot(): lax.dot_general(a, b, (dims, ((), ())), precision=precision, preferred_el...]
    select_n x2, other arithmetic: 4.51 us -> 1.07 us  [the longest x1 0.98 us: body(): packed = jnp.where(column < split, wide_high, rolled)]
  transfers between devices with their start and end apart: 4 -> 12, of which waited for: 4 -> 5; matrix products, arithmetic and copies ran while one was open for 12% -> 21% of each run, Pallas kernels for 0% -> 0%
where the time goes in v1:
time: 89.2 us; the launch traced here: 88.7 us
  waiting for transfers between devices  39.5 us (44%)
  starting transfers between devices  23.9 us (27%)
  other arithmetic  14.8 us (17%)
  matrix products  6.04 us (7%)
  local copies, waits for them, and re-layouts  3.53 us (4%)
    ppermute x10, waiting for transfers between devices, gather_blocks(): lax.ppermute(x, axis, partner_pairs(n, s))  30.6 us
    ppermute x10, starting transfers between devices, gather_blocks(): lax.ppermute(x, axis, partner_pairs(n, s))  15.5 us
    all_to_all x1, waiting for transfers between devices, body(): lax.all_to_all(pieces, 'col', split_axis=0, concat_axis=0, tiled=True)  8.87 us
    another operation x3, other arithmetic, body(): chol = jnp.linalg.cholesky(inner)  6.52 us
    dot_general x5, matrix products, dot(): lax.dot_general(a, b, (dims, ((), ())), precision=precision, preferred_el...  5.61 us
    another operation x2, other arithmetic, body(): factor_t = jax.scipy.linalg.solve_triangular(chol, image_t, lower=True)  5.55 us
    all_to_all x1, starting transfers between devices, body(): lax.all_to_all(pieces, 'col', split_axis=0, concat_axis=0, tiled=True)  4.88 us
    all_to_all x1, starting transfers between devices, body(): lax.all_to_all(packed.reshape(n_col, half, width), 'col', split_axis=0, c...  3.54 us
  transfers between devices with their start and end apart: 12, of which 5 were waited for; matrix products, arithmetic and copies ran while one was open for 21% of the time, Pallas kernels for 0%

profile of v1, /device:TPU:0, one launch (start us, length us, event | category | flops | bytes accessed | tf_op | source)
XLA Modules:
  0.0 88.7 jit_solution(18427996794332701104)
XLA Ops:
  0.7 3.0 %collective-permute-start = (f32[256,512]{1,0:T(8,128)}, f32[256,512]{1,0:T(8,128)}, u32[]{:S(2)}, u32[]{:S(2)}) collective-permute-start(f32[256,512]{1,0:T(8,128)} %param.2), channel_id=1, source_target_pairs={{0,8},{8,0},{16,24},{24,16},{1,9},{9,1},{17,25},{25,17},{2,10},{10... | collective-permute-start | bytes 1572872 | tf_op jit(solution)/shard_map/ppermute | solution.py:26
  3.7 1.5 %collective-permute-start.1 = (f32[256,512]{1,0:T(8,128)}, f32[256,512]{1,0:T(8,128)}, u32[]{:S(2)}, u32[]{:S(2)}) collective-permute-start(f32[256,512]{1,0:T(8,128)} %param.2), channel_id=1, source_target_pairs={{0,16},{8,24},{16,0},{24,8},{1,17},{9,25},{17,1},{25,9},{2,18},{10... | collective-permute-start | bytes 1572872 | tf_op jit(solution)/shard_map/ppermute | solution.py:26
  5.2 0.2 broadcast_in_dim.13
  5.5 11.2 %collective-permute-done = f32[256,512]{1,0:T(8,128)} collective-permute-done((f32[256,512]{1,0:T(8,128)}, f32[256,512]{1,0:T(8,128)}, u32[]{:S(2)}, u32[]{:S(2)}) %collective-permute-start) | collective-permute-done | bytes 524320 | tf_op jit(solution)/shard_map/ppermute | solution.py:26
  16.7 1.1 %constant_dynamic-update-slice_fusion.10 = f32[1024,512]{1,0:T(8,128)S(1)} fusion(f32[1024,512]{1,0:T(8,128)S(1)} %constant_dynamic-update-slice_fusion.11, f32[256,512]{1,0:T(8,128)} %collective-permute-done, s32[]{:T(128)S(6)} %select_n.67), kind=kLoop, calls=%fused_computation.44 | loop fusion | bytes 1048580 | tf_op jit(solution)/shard_map/dynamic_update_slice | solution.py:48
  17.8 10.8 %collective-permute-done.1 = f32[256,512]{1,0:T(8,128)} collective-permute-done((f32[256,512]{1,0:T(8,128)}, f32[256,512]{1,0:T(8,128)}, u32[]{:S(2)}, u32[]{:S(2)}) %collective-permute-start.1) | collective-permute-done | bytes 524320 | tf_op jit(solution)/shard_map/ppermute | solution.py:26
  28.6 1.1 %constant_dynamic-update-slice_fusion.9 = f32[1024,512]{1,0:T(8,128)S(1)} fusion(f32[1024,512]{1,0:T(8,128)S(1)} %constant_dynamic-update-slice_fusion.10, f32[256,512]{1,0:T(8,128)} %collective-permute-done.1, s32[]{:T(128)S(6)} %select_n.68), kind=kLoop, calls=%fused_computation.43 | loop fusion | bytes 1048580 | tf_op jit(solution)/shard_map/dynamic_update_slice | solution.py:48
  29.8 1.1 %convolution_multiply_fusion = f32[256,1024]{1,0:T(8,128)S(1)} fusion(f32[1024,512]{1,0:T(8,128)S(1)} %constant_dynamic-update-slice_fusion.8, f32[128,512]{1,0:T(8,128)S(1)} %get-tuple-element.4, f32[128,512]{1,0:T(8,128)S(1)} %bitcast.30), kind=kOutput, calls=%fused_computation | convolution fusion | flops 805699584 | bytes 3670016 | tf_op jit(solution)/shard_map/dot_general | solution.py:30
  31.0 1.8 %fusion.16 = f32[512,64]{1,0:T(8,128)S(1)} fusion(f32[1024,512]{1,0:T(8,128)S(1)} %constant_dynamic-update-slice_fusion.8, f32[1024,64]{0,1:T(8,128)S(1)} %copy-done), kind=kOutput, calls=%fused_computation.51 | convolution fusion | flops 201326592 | bytes 2490368 | tf_op jit(solution)/shard_map/dot_general | solution.py:30
  32.8 1.1 %fusion = f32[8,8,8,128]{3,2,1,0:T(8,128)S(1)} fusion(f32[512,64]{1,0:T(8,128)S(1)} %fusion.16, f32[1024,512]{1,0:T(8,128)S(1)} %constant_dynamic-update-slice_fusion.8), kind=kOutput, calls=%fused_computation.2 | convolution fusion | flops 201392128 | bytes 2490368 | tf_op jit(solution)/shard_map/dot_general | solution.py:30
  33.9 0.7 copy.10
  34.7 4.9 %all-to-all-start.1 = ((f32[8,64,128]{2,1,0:T(8,128)}), f32[8,64,128]{2,1,0:T(8,128)}, u32[]{:S(2)}, u32[]{:S(2)}) async-start(f32[8,64,128]{2,1,0:T(8,128)} %bitcast.32), calls=%async_computation.1 | async-start | bytes 524288 | tf_op jit(solution)/shard_map/all_to_all | solution.py:53
  39.5 1.0 %fusion.3 = f32[128,1152]{1,0:T(8,128)} fusion(s32[]{:T(128)S(6)} %select_n.72, f32[128,1024]{1,0:T(8,128)S(1)} %get-tuple-element.6, f32[128,128]{1,0:T(8,128)S(1)} %slice.31, f32[128,1024]{1,0:T(8,128)S(1)} %get-tuple-element.5, pred[1152]{0:T(1024)(128)(4,1)S(1)} %iota_compare_fusion.4), kind=kLoop, calls=%fused_computation.9 | loop fusion | flops 442368 | bytes 1705092 | tf_op jit(solution)/shard_map/jit(_where)/select_n | solution.py:78
  40.5 8.9 %all-to-all-done.1 = f32[8,64,128]{2,1,0:T(8,128)} async-done(((f32[8,64,128]{2,1,0:T(8,128)}), f32[8,64,128]{2,1,0:T(8,128)}, u32[]{:S(2)}, u32[]{:S(2)}) %all-to-all-start.1) | async-done | bytes 262176 | tf_op jit(solution)/shard_map/all_to_all | solution.py:53
  49.4 3.5 %all-to-all-start = ((f32[8,16,1152]{2,1,0:T(8,128)}), f32[8,16,1152]{2,1,0:T(8,128)S(1)}, u32[]{:S(2)}, u32[]{:S(2)}) async-start(f32[8,16,1152]{2,1,0:T(8,128)} %bitcast.2), calls=%async_computation | async-start | bytes 1179648 | tf_op jit(solution)/shard_map/all_to_all | solution.py:79
  52.9 1.0 %reduce_sum.19 = f32[64,128]{1,0:T(8,128)S(1)} reduce(f32[8,64,128]{2,1,0:T(8,128)} %all-to-all-done.1, f32[]{:T(128)} %constant.78.clone.1), dimensions={0}, to_apply=%region_1.2 | reduce | flops 57344 | bytes 294916 | tf_op jit(solution)/shard_map/reduce_sum | solution.py:54
  53.9 0.5 collective-permute-start.3
  54.4 1.7 %collective-permute-start.4 = (f32[64,128]{1,0:T(8,128)S(1)}, f32[64,128]{1,0:T(8,128)S(1)}, u32[]{:S(2)}, u32[]{:S(2)}) collective-permute-start(f32[64,128]{1,0:T(8,128)S(1)} %reduce_sum.19), channel_id=1, source_target_pairs={{0,2},{1,3},{2,0},{3,1},{4,6},{5,7},{6,4},{7,5},{8,10},{9,11},{10,... | collective-permute-start | bytes 98312 | tf_op jit(solution)/shard_map/ppermute | solution.py:26
  56.1 2.6 %collective-permute-start.6 = (f32[64,128]{1,0:T(8,128)S(1)}, f32[64,128]{1,0:T(8,128)S(1)}, u32[]{:S(2)}, u32[]{:S(2)}) collective-permute-start(f32[64,128]{1,0:T(8,128)S(1)} %reduce_sum.19), channel_id=1, source_target_pairs={{0,4},{1,5},{2,6},{3,7},{4,0},{5,1},{6,2},{7,3},{8,12},{9,13},{10,... | collective-permute-start | bytes 98312 | tf_op jit(solution)/shard_map/ppermute | solution.py:26
  58.7 0.1 collective-permute-start.7
  58.8 3.6 %collective-permute-start.8 = (f32[64,128]{1,0:T(8,128)S(1)}, f32[64,128]{1,0:T(8,128)S(1)}, u32[]{:S(2)}, u32[]{:S(2)}) collective-permute-start(f32[64,128]{1,0:T(8,128)S(1)} %reduce_sum.19), channel_id=1, source_target_pairs={{0,6},{1,7},{2,4},{3,5},{4,2},{5,3},{6,0},{7,1},{8,14},{9,15},{10,... | collective-permute-start | bytes 98312 | tf_op jit(solution)/shard_map/ppermute | solution.py:26
  62.4 2.0 %collective-permute-done.4 = f32[64,128]{1,0:T(8,128)S(1)} collective-permute-done((f32[64,128]{1,0:T(8,128)S(1)}, f32[64,128]{1,0:T(8,128)S(1)}, u32[]{:S(2)}, u32[]{:S(2)}) %collective-permute-start.4) | collective-permute-done | bytes 32800 | tf_op jit(solution)/shard_map/ppermute | solution.py:26
  64.4 2.5 %collective-permute-start.9 = (f32[64,128]{1,0:T(8,128)S(1)}, f32[64,128]{1,0:T(8,128)S(1)}, u32[]{:S(2)}, u32[]{:S(2)}) collective-permute-start(f32[64,128]{1,0:T(8,128)S(1)} %reduce_sum.19), channel_id=1, source_target_pairs={{0,7},{1,6},{2,5},{3,4},{4,3},{5,2},{6,1},{7,0},{8,15},{9,14},{10,... | collective-permute-start | bytes 98312 | tf_op jit(solution)/shard_map/ppermute | solution.py:26
  67.0 6.6 %collective-permute-done.6 = f32[64,128]{1,0:T(8,128)S(1)} collective-permute-done((f32[64,128]{1,0:T(8,128)S(1)}, f32[64,128]{1,0:T(8,128)S(1)}, u32[]{:S(2)}, u32[]{:S(2)}) %collective-permute-start.6) | collective-permute-done | bytes 32800 | tf_op jit(solution)/shard_map/ppermute | solution.py:26
  73.7 0.4 fusion.17
  74.2 5.8 %cholesky.16 = f32[64,64]{1,0:T(8,128)S(1)} custom-call(f32[64,64]{1,0:T(8,128)S(1)} %fusion.12), custom_call_target="Cholesky" | custom-call | tf_op jit(solution)/shard_map/jit(cholesky)/cholesky | solution.py:60
  80.0 0.6 compare_reduce_fusion
  80.7 0.7 fusion.9
  81.3 4.9 %custom-call.7 = f32[1,64,64]{1,2,0:T(8,128)S(1)} custom-call(f32[1,64,64]{2,1,0:T(8,128)S(1)} %fusion.9), custom_call_target="InvertDiagBlocksLowerTriangular" | custom-call | tf_op jit(solution)/shard_map/jit(_solve_triangular)/triangular_solve | solution.py:61
  86.2 0.4 fusion.10
  86.7 1.2 %convolution_multiply_fusion.2 = f32[16,512]{1,0:T(8,128)} fusion(f32[1024,512]{1,0:T(8,128)S(1)} %constant_dynamic-update-slice_fusion.8, f32[64,1024]{1,0:T(8,128)S(1)} %fusion.10, s32[]{:T(128)S(6)} %select_n.86), kind=kOutput, calls=%fused_computation.6 | convolution fusion | flops 50339840 | bytes 2195460 | tf_op jit(solution)/shard_map/dot_general | solution.py:30
  88.1 0.7 pad_maximum_fusion
  (37 shorter events, 0.6 us)
Async XLA Ops:
  0.6 30.4 %copy-start = (f32[1024,64]{0,1:T(8,128)S(1)}, f32[1024,64]{0,1:T(8,128)}, u32[]{:S(2)}) copy-start(f32[1024,64]{0,1:T(8,128)} %param.3) | copy-start | bytes 786436
  0.6 4.8 %copy-start.1 = (f32[256,512]{1,0:T(8,128)S(1)}, f32[256,512]{1,0:T(8,128)}, u32[]{:S(2)}) copy-start(f32[256,512]{1,0:T(8,128)} %param.2) | copy-start | bytes 1572868
  0.7 16.1 %collective-permute-start = (f32[256,512]{1,0:T(8,128)}, f32[256,512]{1,0:T(8,128)}, u32[]{:S(2)}, u32[]{:S(2)}) collective-permute-start(f32[256,512]{1,0:T(8,128)} %param.2), channel_id=1, source_target_pairs={{0,8},{8,0},{16,24},{24,16},{1,9},{9,1},{17,25},{25,17},{2,10},{10... | collective-permute-start | bytes 1572872 | tf_op jit(solution)/shard_map/ppermute | solution.py:26
  3.7 24.9 %collective-permute-start.1 = (f32[256,512]{1,0:T(8,128)}, f32[256,512]{1,0:T(8,128)}, u32[]{:S(2)}, u32[]{:S(2)}) collective-permute-start(f32[256,512]{1,0:T(8,128)} %param.2), channel_id=1, source_target_pairs={{0,16},{8,24},{16,0},{24,8},{1,17},{9,25},{17,1},{25,9},{2,18},{10... | collective-permute-start | bytes 1572872 | tf_op jit(solution)/shard_map/ppermute | solution.py:26
  5.2 24.5 %collective-permute-start.2 = (f32[256,512]{1,0:T(8,128)}, f32[256,512]{1,0:T(8,128)S(1)}, u32[]{:S(2)}, u32[]{:S(2)}) collective-permute-start(f32[256,512]{1,0:T(8,128)} %param.2), channel_id=1, source_target_pairs={{0,24},{8,16},{16,8},{24,0},{1,25},{9,17},{17,9},{25,1},{2,26},{10... | collective-permute-start | bytes 1572872 | tf_op jit(solution)/shard_map/ppermute | solution.py:26
  34.7 14.7 %all-to-all-start.1 = ((f32[8,64,128]{2,1,0:T(8,128)}), f32[8,64,128]{2,1,0:T(8,128)}, u32[]{:S(2)}, u32[]{:S(2)}) async-start(f32[8,64,128]{2,1,0:T(8,128)} %bitcast.32), calls=%async_computation.1 | async-start | bytes 524288 | tf_op jit(solution)/shard_map/all_to_all | solution.py:53
  49.4 38.5 %all-to-all-start = ((f32[8,16,1152]{2,1,0:T(8,128)}), f32[8,16,1152]{2,1,0:T(8,128)S(1)}, u32[]{:S(2)}, u32[]{:S(2)}) async-start(f32[8,16,1152]{2,1,0:T(8,128)} %bitcast.2), calls=%async_computation | async-start | bytes 1179648 | tf_op jit(solution)/shard_map/all_to_all | solution.py:79
  53.9 4.9 %collective-permute-start.3 = (f32[64,128]{1,0:T(8,128)S(1)}, f32[64,128]{1,0:T(8,128)S(1)}, u32[]{:S(2)}, u32[]{:S(2)}) collective-permute-start(f32[64,128]{1,0:T(8,128)S(1)} %reduce_sum.19), channel_id=1, source_target_pairs={{0,1},{1,0},{2,3},{3,2},{4,5},{5,4},{6,7},{7,6},{8,9},{9,8},{10,11... | collective-permute-start | bytes 98312 | tf_op jit(solution)/shard_map/ppermute | solution.py:26
  54.4 10.0 %collective-permute-start.4 = (f32[64,128]{1,0:T(8,128)S(1)}, f32[64,128]{1,0:T(8,128)S(1)}, u32[]{:S(2)}, u32[]{:S(2)}) collective-permute-start(f32[64,128]{1,0:T(8,128)S(1)} %reduce_sum.19), channel_id=1, source_target_pairs={{0,2},{1,3},{2,0},{3,1},{4,6},{5,7},{6,4},{7,5},{8,10},{9,11},{10,... | collective-permute-start | bytes 98312 | tf_op jit(solution)/shard_map/ppermute | solution.py:26
  56.1 10.9 %collective-permute-start.5 = (f32[64,128]{1,0:T(8,128)S(1)}, f32[64,128]{1,0:T(8,128)S(1)}, u32[]{:S(2)}, u32[]{:S(2)}) collective-permute-start(f32[64,128]{1,0:T(8,128)S(1)} %reduce_sum.19), channel_id=1, source_target_pairs={{0,3},{1,2},{2,1},{3,0},{4,7},{5,6},{6,5},{7,4},{8,11},{9,10},{10,... | collective-permute-start | bytes 98312 | tf_op jit(solution)/shard_map/ppermute | solution.py:26
  56.1 17.5 %collective-permute-start.6 = (f32[64,128]{1,0:T(8,128)S(1)}, f32[64,128]{1,0:T(8,128)S(1)}, u32[]{:S(2)}, u32[]{:S(2)}) collective-permute-start(f32[64,128]{1,0:T(8,128)S(1)} %reduce_sum.19), channel_id=1, source_target_pairs={{0,4},{1,5},{2,6},{3,7},{4,0},{5,1},{6,2},{7,3},{8,12},{9,13},{10,... | collective-permute-start | bytes 98312 | tf_op jit(solution)/shard_map/ppermute | solution.py:26
  58.7 14.9 %collective-permute-start.7 = (f32[64,128]{1,0:T(8,128)S(1)}, f32[64,128]{1,0:T(8,128)S(1)}, u32[]{:S(2)}, u32[]{:S(2)}) collective-permute-start(f32[64,128]{1,0:T(8,128)S(1)} %reduce_sum.19), channel_id=1, source_target_pairs={{0,5},{1,4},{2,7},{3,6},{4,1},{5,0},{6,3},{7,2},{8,13},{9,12},{10,... | collective-permute-start | bytes 98312 | tf_op jit(solution)/shard_map/ppermute | solution.py:26
  58.8 14.8 %collective-permute-start.8 = (f32[64,128]{1,0:T(8,128)S(1)}, f32[64,128]{1,0:T(8,128)S(1)}, u32[]{:S(2)}, u32[]{:S(2)}) collective-permute-start(f32[64,128]{1,0:T(8,128)S(1)} %reduce_sum.19), channel_id=1, source_target_pairs={{0,6},{1,7},{2,4},{3,5},{4,2},{5,3},{6,0},{7,1},{8,14},{9,15},{10,... | collective-permute-start | bytes 98312 | tf_op jit(solution)/shard_map/ppermute | solution.py:26
  64.4 9.3 %collective-permute-start.9 = (f32[64,128]{1,0:T(8,128)S(1)}, f32[64,128]{1,0:T(8,128)S(1)}, u32[]{:S(2)}, u32[]{:S(2)}) collective-permute-start(f32[64,128]{1,0:T(8,128)S(1)} %reduce_sum.19), channel_id=1, source_target_pairs={{0,7},{1,6},{2,5},{3,4},{4,3},{5,2},{6,1},{7,0},{8,15},{9,14},{10,... | collective-permute-start | bytes 98312 | tf_op jit(solution)/shard_map/ppermute | solution.py:26
  86.7 2.1 %copy-start.2 = (f32[64,1024]{1,0:T(8,128)}, f32[64,1024]{1,0:T(8,128)S(1)}, u32[]{:S(2)}) copy-start(f32[64,1024]{1,0:T(8,128)S(1)} %fusion.10) | copy-start | bytes 786436
